TPU v7x, 256 devices: a whole 4x4x8 slice. The times are simulated.
256 devices in a mesh: dom: 128 (over x, y_hi, z, core), feat: 2 (over y_lo).
Axes of the slice: x: 4, y: 4 (y_hi: 2, y_lo: 2; y = y_hi * 2 + y_lo), z: 8, core: 2. Of those that a mesh axis runs over, the one named last changes fastest.
Arguments:
- features: float32 [131072, 512], P('dom', 'feat'), may hold values from -6 to 6
- weight: float32 [512, 512], P(None, 'feat'), may hold values from -0.25 to 0.25
- cotangent: float32 [131072, 512], P('dom', 'feat'), may hold values from -6 to 6
- block_rows: int32 [128, 4, 24], P('dom'), may hold values from 0 to 7, as said below
- block_cols: int32 [128, 4, 24], P('dom'), may hold values from 0 to 7, as said below
- block_counts: int32 [128, 4], P('dom'), may hold values from 1 to 24, as said below
- block_values: float32 [128, 4, 24, 128, 128], P('dom'), may hold values from -0.25 to 0.25
Outputs:
- activated: float32 [131072, 512], P('dom', 'feat')
- feature_grad: float32 [131072, 512], P('dom', 'feat')
- weight_grad: float32 [512, 512], P(None, 'feat')
Inputs may be any that keep to these rules, and one draw needn't show every extreme that they name: `block_rows`: every entry is below 8; within one partition and slot the pairs (block_rows, block_cols) are all different. `block_cols`: every entry is below 8. `block_counts`: some partition has 24 blocks in every slot.
All inputs are finite; a program needn't handle non-finite values.
Results may differ from a plain program's by a relative error of at most 0.0003.
Values sent between devices are 32-bit elements; how exact they have to be, the bound alone decides.
A program may use at most 128 MiB of HBM per device.

v0:
```python
import math

import jax
import jax.numpy as jnp
from jax import lax
from jax.sharding import PartitionSpec as P


def passed_along(value, axis, by):
    peers = lax.axis_size(axis)
    return lax.ppermute(value, axis, [(i, (i + by) % peers) for i in range(peers)])


def slot_forward(slot_index, source, row_pick, col_pick, blocks):
    block_count = row_pick.shape[-1]
    gridded = source.reshape(block_count, -1, source.shape[-1])
    picked = jnp.einsum(
        "cr,rbh->cbh", col_pick[slot_index], gridded, precision=lax.Precision.HIGHEST
    )
    product = jnp.einsum(
        "cij,cjh->cih", blocks[slot_index], picked, precision=lax.Precision.HIGHEST
    )
    placed = jnp.einsum(
        "cr,cih->rih", row_pick[slot_index], product, precision=lax.Precision.HIGHEST
    )
    return placed.reshape(source.shape)


def slot_backward(slot_index, incoming, row_pick, col_pick, blocks):
    block_count = row_pick.shape[-1]
    gridded = incoming.reshape(block_count, -1, incoming.shape[-1])
    picked = jnp.einsum(
        "cr,rih->cih", row_pick[slot_index], gridded, precision=lax.Precision.HIGHEST
    )
    product = jnp.einsum(
        "cij,cih->cjh", blocks[slot_index], picked, precision=lax.Precision.HIGHEST
    )
    placed = jnp.einsum(
        "cr,cjh->rjh", col_pick[slot_index], product, precision=lax.Precision.HIGHEST
    )
    return placed.reshape(incoming.shape)


def body(features, weight, cotangent, block_rows, block_cols, block_counts, block_values):
    rows_here = features.shape[0]
    block_size = block_values.shape[-1]
    block_count = rows_here // block_size
    window = block_values.shape[1]
    capacity = block_values.shape[2]
    full_rows = lax.all_gather(features, "feat", axis=1, tiled=True)
    hidden = jnp.dot(
        full_rows, weight, precision=lax.Precision.HIGHEST, preferred_element_type=jnp.float32
    )
    live = (jnp.arange(capacity, dtype=jnp.int32)[None, :] < block_counts[0][:, None]).astype(
        jnp.float32
    )
    blocks = block_values[0] * live[:, :, None, None]
    targets = jnp.arange(block_count, dtype=jnp.int32)
    row_pick = (block_rows[0][:, :, None] == targets).astype(jnp.float32)
    col_pick = (block_cols[0][:, :, None] == targets).astype(jnp.float32)
    pre = slot_forward(0, hidden, row_pick, col_pick, blocks)
    current = hidden
    for slot_index in range(1, window):
        current = passed_along(current, "dom", 1)
        pre = pre + slot_forward(slot_index, current, row_pick, col_pick, blocks)
    activated = jax.nn.silu(pre)
    sigmoid_pre = jax.nn.sigmoid(pre)
    pre_grad = cotangent * (sigmoid_pre + pre * sigmoid_pre * (1.0 - sigmoid_pre))
    carried = slot_backward(window - 1, pre_grad, row_pick, col_pick, blocks)
    for slot_index in range(window - 2, -1, -1):
        carried = passed_along(carried, "dom", -1)
        carried = carried + slot_backward(slot_index, pre_grad, row_pick, col_pick, blocks)
    local_weight = jnp.einsum("nk,nh->kh", full_rows, carried, precision=lax.Precision.HIGHEST)
    summed_weight = lax.psum(local_weight, "dom")
    weight_grad = summed_weight * jnp.float32(1.0 / math.sqrt(rows_here * lax.axis_size("dom")))
    partial_grad = jnp.einsum("nh,kh->nk", carried, weight, precision=lax.Precision.HIGHEST)
    feature_grad = lax.psum_scatter(partial_grad, "feat", scatter_dimension=1, tiled=True)
    return (activated, feature_grad, weight_grad)


def solution(mesh):
    in_specs = (
        P("dom", "feat"),
        P(None, "feat"),
        P("dom", "feat"),
        P("dom", None, None),
        P("dom", None, None),
        P("dom", None),
        P("dom", None, None, None, None),
    )
    out_specs = (P("dom", "feat"), P("dom", "feat"), P(None, "feat"))
    return jax.shard_map(body, mesh=mesh, in_specs=in_specs, out_specs=out_specs, check_vma=False)
```

profile of v0, /device:TPU:22, one launch (start us, length us, event | category | flops | bytes accessed | tf_op | source)
XLA Modules:
  0.0 1413.3 jit_solution(4753553223223909049)
XLA Ops:
  8.7 5.9 bitcast_multiply_fusion
  14.6 35.9 %all-gather.2.cloned.1.call-done = f32[1024,512]{1,0:T(8,128)} async-done(((f32[1024,256]{1,0:T(8,128)}), f32[1024,512]{1,0:T(8,128)}) %all-gather.2.cloned.1.call-update) | async-done | bytes 2097168 | tf_op jit(solution)/shard_map/all_gather | solution.py:50
  50.5 3.5 fusion.61
  55.9 3.8 fusion.30
  59.7 12.2 collective-permute-done
  73.9 3.8 fusion.26
  80.6 9.4 collective-permute-done.1
  91.9 3.8 fusion.22
  98.6 9.4 collective-permute-done.2
  109.7 4.2 fusion.18
  116.9 3.1 fusion.38
  123.4 4.1 fusion.14
  133.7 3.9 fusion.10
  137.7 2.9 fusion.8
  140.9 3.4 collective-permute-done.3
  144.4 6.0 collective-permute-start.4
  152.2 3.9 fusion.6
  159.4 3.4 collective-permute-done.4
  162.9 5.8 collective-permute-start.5
  170.4 3.9 fusion.2
  177.6 3.4 collective-permute-done.5
  184.0 3.2 fusion.62
  187.2 1131.0 %all-reduce.2.cloned.1.call-done = f32[512,256]{0,1:T(8,128)} async-done(((f32[512,256]{0,1:T(8,128)}), f32[512,256]{0,1:T(8,128)}) %all-reduce.2.cloned.1.call-update) | async-done | bytes 524304 | tf_op jit(solution)/shard_map/psum | solution.py:74
  1320.3 86.4 %reduce-scatter.2.cloned.1.call-done = f32[1024,256]{1,0:T(8,128)} async-done(((f32[1024,512]{1,0:T(8,128)}), f32[1024,256]{1,0:T(8,128)}) %reduce-scatter.2.cloned.1.call-update) | async-done | bytes 1048592 | tf_op jit(solution)/shard_map/reduce_scatter | solution.py:77
  (51 shorter events, 43.0 us)
Async XLA Ops:
  7.2 43.3 %copy-start = (f32[512,256]{1,0:T(8,128)S(1)}, f32[512,256]{1,0:T(8,128)}, u32[]{:S(2)}) copy-start(f32[512,256]{1,0:T(8,128)} %param.8) | copy-start | bytes 1572868
  7.2 43.3 %all-gather.2.cloned.1.call-start = ((), (), s32[]{:S(2)}) async-start(), calls=%async_computation.1 | async-start | bytes 3145728 | tf_op jit(solution)/shard_map/all_gather | solution.py:50
  7.9 1310.2 %all-reduce.2.cloned.1.call-start = ((), (), s32[]{:S(2)}) async-start(), calls=%async_computation.3 | async-start | bytes 1048576 | tf_op jit(solution)/shard_map/psum | solution.py:74
  14.6 39.5 %copy-start.4 = (s32[1,4,24]{2,1,0:T(4,128)S(1)}, s32[1,4,24]{2,1,0:T(4,128)}, u32[]{:S(2)}) copy-start(s32[1,4,24]{2,1,0:T(4,128)} %param.11) | copy-start | bytes 1156
  14.6 39.5 %copy-start.5 = (s32[1,4,24]{2,1,0:T(4,128)S(1)}, s32[1,4,24]{2,1,0:T(4,128)}, u32[]{:S(2)}) copy-start(s32[1,4,24]{2,1,0:T(4,128)} %param.10) | copy-start | bytes 1156
  50.5 5.4 copy-start.1
  54.0 17.9 %collective-permute-start = (f32[1024,256]{1,0:T(8,128)S(1)}, f32[1024,256]{1,0:T(8,128)S(1)}, u32[]{:S(2)}, u32[]{:S(2)}) collective-permute-start(f32[1024,256]{1,0:T(8,128)S(1)} %fusion.61), channel_id=1, source_target_pairs={{0,2},{2,4},{4,6},{6,8},{8,10},{10,12},{12,14},{14,16},{16,18},{18... | collective-permute-start | bytes 3145736 | tf_op jit(solution)/shard_map/ppermute | solution.py:11
  72.0 18.0 %collective-permute-start.1 = (f32[1024,256]{1,0:T(8,128)S(1)}, f32[1024,256]{1,0:T(8,128)S(1)}, u32[]{:S(2)}, u32[]{:S(2)}) collective-permute-start(f32[1024,256]{1,0:T(8,128)S(1)} %collective-permute-done), channel_id=1, source_target_pairs={{0,2},{2,4},{4,6},{6,8},{8,10},{10,12},{12,14},{14,16},{16,18},{18... | collective-permute-start | bytes 3145736 | tf_op jit(solution)/shard_map/ppermute | solution.py:11
  89.9 18.0 %collective-permute-start.2 = (f32[1024,256]{1,0:T(8,128)S(1)}, f32[1024,256]{1,0:T(8,128)S(1)}, u32[]{:S(2)}, u32[]{:S(2)}) collective-permute-start(f32[1024,256]{1,0:T(8,128)S(1)} %collective-permute-done.1), channel_id=1, source_target_pairs={{0,2},{2,4},{4,6},{6,8},{8,10},{10,12},{12,14},{14,16},{16,18},{18... | collective-permute-start | bytes 3145736 | tf_op jit(solution)/shard_map/ppermute | solution.py:11
  116.8 3.4 copy-start.3
  130.7 13.5 collective-permute-start.3
  144.4 18.3 %collective-permute-start.4 = (f32[1024,256]{1,0:T(8,128)S(1)}, f32[1024,256]{1,0:T(8,128)S(1)}, u32[]{:S(2)}, u32[]{:S(2)}) collective-permute-start(f32[1024,256]{1,0:T(8,128)S(1)} %bitcast_add_fusion.2), channel_id=1, source_target_pairs={{0,254},{2,0},{4,2},{6,4},{8,6},{10,8},{12,10},{14,12},{16,14},{18... | collective-permute-start | bytes 3145736 | tf_op jit(solution)/shard_map/ppermute | solution.py:11
  162.9 18.1 %collective-permute-start.5 = (f32[1024,256]{1,0:T(8,128)S(1)}, f32[1024,256]{1,0:T(8,128)S(1)}, u32[]{:S(2)}, u32[]{:S(2)}) collective-permute-start(f32[1024,256]{1,0:T(8,128)S(1)} %bitcast_add_fusion.1), channel_id=1, source_target_pairs={{0,254},{2,0},{4,2},{6,4},{8,6},{10,8},{12,10},{14,12},{16,14},{18... | collective-permute-start | bytes 3145736 | tf_op jit(solution)/shard_map/ppermute | solution.py:11
  177.3 3.9 copy-start.2
  183.9 1222.7 %reduce-scatter.2.cloned.1.call-start = ((), (), s32[]{:S(2)}) async-start(), calls=%async_computation.2 | async-start | bytes 3145728 | tf_op jit(solution)/shard_map/reduce_scatter | solution.py:77
Sparse Core Ops, SparseCore 0:
  9.8 40.6 all-gather.1
  184.0 1134.0 all-reduce.1
  1321.4 85.1 reduce-scatter.1
where the time goes:
time: 1420 us; the launch traced here: 1410 us
  waiting for transfers between devices  1290 us (91%)
  matrix products  78.3 us (6%)
  between operations  14.3 us (1%)
    psum x1, waiting for transfers between devices, body(): summed_weight = lax.psum(local_weight, 'dom')  1130 us
    reduce_scatter x1, waiting for transfers between devices, body(): lax.psum_scatter(partial_grad, 'feat', scatter_dimension=1, tiled=True)  86.4 us
    ppermute x6, waiting for transfers between devices, passed_along(): lax.ppermute(value, axis, [(i, (i + by) % peers) for i in range(peers)])  41 us
    all_gather x1, waiting for transfers between devices, body(): full_rows = lax.all_gather(features, 'feat', axis=1, tiled=True)  35.9 us
  transfers between devices with their start and end apart: 9, of which 9 were waited for; matrix products, arithmetic and copies ran while one was open for 4% of the time, Pallas kernels for 0%

commit v1 on v0

v1 whole, which is shorter than its diff:
```python
import math

import jax
import jax.numpy as jnp
from jax import lax
from jax.experimental import pallas as pl
from jax.experimental.pallas import tpu as pltpu
from jax.sharding import PartitionSpec as P

MESH = pl.DeviceIdType.MESH
F32 = jnp.float32
BF16 = jnp.bfloat16
X, Y, Z, CORES = 4, 2, 8, 2
PARTS = X * Y * Z * CORES
SLOTS, CAP, GRID = 4, 24, 8
ROWS, HALF, LANES = 1024, 256, 128


def split(value):
    high = value.astype(BF16)
    return high, (value - high.astype(F32)).astype(BF16)


def dot(a, b):
    return jnp.dot(a, b, preferred_element_type=F32)


def dot3(a, b):
    return dot(a[0], b[0]) + dot(a[1], b[0]) + dot(a[0], b[1])


def remote(src, dst, send, recv, device):
    return pltpu.make_async_remote_copy(
        src_ref=src, dst_ref=dst, send_sem=send, recv_sem=recv,
        device_id=device, device_id_type=MESH,
    )


def kernel(
    table, features, weight, cotangent, blocks_in,
    act_out, grad_out, wgrad_out,
    blocks, adj_hi, adj_lo, own, w_raw, w_hi, w_lo, wt_hi, wt_lo, cot,
    fwd, agg, agg_far, pre, act, pgt_hi, pgt_lo,
    z_send, z_recv, f_send, f_recv, f_own,
    ar, ar_core, s1, ar_x, s2, ar_y, s3, ar_z, ag, wg,
    local_sem, fwd_ss, fwd_rs, y_ss, y_rs, z_ss, z_rs, f_ss, f_rs,
    ar_ss, ar_rs, ag_ss, ag_rs,
):
    me = lax.axis_index("dom")
    feat = lax.axis_index("feat")
    other = 1 - feat
    core = lax.rem(me, 2)
    z = lax.rem(me // 2, Z)
    y = lax.rem(me // (2 * Z), Y)
    x = me // (2 * Z * Y)
    up = (lax.rem(me + 1, PARTS), feat)
    down = (lax.rem(me + PARTS - 1, PARTS), feat)
    mate = (me, other)

    def at(x_, y_, z_, core_):
        return (((x_ * Y + y_) * Z + z_) * 2 + core_, feat)

    core_peer = at(x, y, z, 1 - core)
    y_peer = at(x, 1 - y, z, core)

    def x_peer(d):
        return lax.rem(x + d, X)

    def z_peer(d):
        return lax.rem(z + d, Z)

    loads = [
        pltpu.make_async_copy(blocks_in, blocks, local_sem.at[0]),
        pltpu.make_async_copy(features, own, local_sem.at[1]),
        pltpu.make_async_copy(weight, w_raw, local_sem.at[2]),
        pltpu.make_async_copy(cotangent, cot, local_sem.at[3]),
    ]
    for load in loads:
        load.start()

    barrier = pltpu.get_barrier_semaphore()
    partners = [up, down, mate, y_peer]
    partners += [at(x_peer(d), y, z, core) for d in range(1, X)]
    partners += [at(x, y, z_peer(d), core) for d in range(1, Z)]
    for partner in partners:
        pl.semaphore_signal(barrier, inc=1, device_id=partner, device_id_type=MESH)
    pl.semaphore_wait(barrier, len(partners))

    def fwd_at(w, c, j):
        return ((w - 1) * 2 + c) * 4 + j

    def fwd_copy(w, c, j):
        i = fwd_at(w, c, j)
        if w == 1:
            src = features.at[pl.ds(j * 256, 256), pl.ds(c * LANES, LANES)]
        else:
            src = fwd.at[fwd_at(w - 1, c, j)]
        return remote(src, fwd.at[i], fwd_ss.at[i], fwd_rs.at[i], up)

    def each(n, body, start=0):
        def step(j, carry):
            body(j)
            return carry

        lax.fori_loop(start, start + n, step, 0)

    def send_own(c):
        for j in range(4):
            fwd_copy(1, c, j).start()

    def pass_on(w, c):
        def body(j):
            fwd_copy(w, c, j).wait_recv()
            fwd_copy(w + 1, c, j).start()

        each(4, body)

    def densify(w):
        def body(r):
            rows = pl.ds(pl.multiple_of(r * LANES, LANES), LANES)
            for c in range(GRID):
                found = table[(w * GRID + r) * GRID + c]
                live = jnp.where(found >= 0, 1.0, 0.0).astype(F32)
                high, low = split(blocks[w * CAP + jnp.maximum(found, 0)] * live)
                adj_hi[w * GRID + c, rows, :] = high
                adj_lo[w * GRID + c, rows, :] = low

        each(GRID, body)

    def gather_in(w, c, j, piece, first=False, last=None):
        high, low = split(piece)
        both = jnp.concatenate([high, low], axis=1)

        def body(i):
            rows = pl.ds(pl.multiple_of(i * 512, 512), 512)
            a_hi = jnp.concatenate(
                [adj_hi[w * GRID + 2 * j, rows, :], adj_hi[w * GRID + 2 * j + 1, rows, :]], axis=1
            )
            a_lo = jnp.concatenate(
                [adj_lo[w * GRID + 2 * j, rows, :], adj_lo[w * GRID + 2 * j + 1, rows, :]], axis=1
            )
            wide = dot(a_hi, both)
            total = wide[:, :LANES] + wide[:, LANES:] + dot(a_lo, high)
            if first:
                agg[c, rows, :] = total
            else:
                agg[c, rows, :] += total
            if last is not None:
                last(i)

        each(2, body)

    def gather_own(c):
        def piece(j):
            rows = pl.ds(pl.multiple_of(j * 256, 256), 256)
            return own[rows, pl.ds(c * LANES, LANES)]

        gather_in(0, c, 0, piece(0), first=True)
        each(3, lambda j: gather_in(0, c, j, piece(j)), 1)

    def gather_slot(w, c, wait, n=4):
        def body(j):
            if wait:
                fwd_copy(w, c, j).wait_recv()
            gather_in(w, c, j, fwd[fwd_at(w, c, j)])

        each(n, body)

    def y_copy(c, i):
        rows = pl.ds(pl.multiple_of(i * 512, 512), 512)
        n = c * 2 + i
        return remote(agg.at[c, rows], agg_far.at[c, rows], y_ss.at[n], y_rs.at[n], mate)

    def gather_last(c):
        gather_slot(3, c, True, 3)
        fwd_copy(3, c, 3).wait_recv()
        gather_in(3, c, 3, fwd[fwd_at(3, c, 3)], last=lambda i: y_copy(c, i).start())

    send_own(0)
    loads[0].wait()
    densify(0)
    densify(1)
    pass_on(1, 0)
    densify(2)
    pass_on(2, 0)
    send_own(1)
    densify(3)
    loads[1].wait()
    gather_own(0)
    gather_slot(1, 0, False)
    gather_slot(2, 0, False)
    pass_on(1, 1)
    gather_last(0)
    pass_on(2, 1)
    gather_own(1)
    gather_slot(1, 1, False)
    gather_slot(2, 1, False)

    loads[2].wait()
    for k in range(2):
        value = w_raw[pl.ds(k * HALF, HALF), :]
        w_hi[k], w_lo[k] = split(value)
        wt_hi[k], wt_lo[k] = split(value.T)
    loads[3].wait()
    gather_last(1)

    def near_part(i):
        rows = pl.ds(pl.multiple_of(i * 256, 256), 256)
        value = jnp.concatenate([agg[0, rows, :], agg[1, rows, :]], axis=1)
        pre[rows, :] = dot3(split(value), (w_hi[feat], w_lo[feat]))

    each(4, near_part)
    for i in range(2):
        y_copy(0, i).wait_recv()

    def far_part(c, i):
        rows = pl.ds(pl.multiple_of(i * 256, 256), 256)
        ks = pl.ds(c * LANES, LANES)
        return dot3(split(agg_far[c, rows, :]), (w_hi[other, ks, :], w_lo[other, ks, :]))

    def far_first(i):
        rows = pl.ds(pl.multiple_of(i * 256, 256), 256)
        pre[rows, :] += far_part(0, i)

    each(4, far_first)

    def activate(i):
        rows = pl.ds(pl.multiple_of(i * 256, 256), 256)
        value = pre[rows, :] + far_part(1, i)
        s = jax.nn.sigmoid(value)
        act[rows, :] = value * s
        grad = cot[rows, :] * (s + value * s * (1.0 - s))
        pgt_hi[:, rows], pgt_lo[:, rows] = split(grad.T)

    for i in range(2):
        y_copy(1, i).wait_recv()
        each(2, activate, 2 * i)
    act_copy = pltpu.make_async_copy(act, act_out, local_sem.at[4])
    act_copy.start()

    def term(w, j):
        n = w * GRID + j
        high, low = pgt_hi[...], pgt_lo[...]
        return dot(high, adj_hi[n]) + dot(low, adj_hi[n]) + dot(high, adj_lo[n])

    def z_copy(s, j):
        n = s * GRID + j
        return remote(z_send.at[n], z_recv.at[n], z_ss.at[n], z_rs.at[n], down)

    def z_step(s, j):
        value = term(3 - s, j)
        if s > 0:
            z_copy(s - 1, j).wait_recv()
            value = value + z_recv[(s - 1) * GRID + j]
        z_send[s * GRID + j] = value
        z_copy(s, j).start()

    def f_copy(j):
        return remote(f_send.at[j], f_recv.at[j], f_ss.at[j], f_rs.at[j], mate)

    def last_step(j):
        value = term(0, j)
        z_copy(2, j).wait_recv()
        value = value + z_recv[2 * GRID + j]
        parts = split(value.T)
        f_send[j] = dot3(parts, (wt_hi[other], wt_lo[other]))
        f_copy(j).start()
        f_own[j] = dot3(parts, (wt_hi[feat], wt_lo[feat]))

    scale = F32(1.0 / math.sqrt(ROWS * PARTS))

    def weight_part(source, half, c):
        grad = dot3((pgt_hi[...], pgt_lo[...]), split(source[c])).T * scale
        for h in range(2):
            start = pl.multiple_of(h * 512 + half * HALF + c * LANES, LANES)
            ar[pl.ds(start, LANES), :] = grad[:, h * LANES:(h + 1) * LANES]

    def rows_at(start, size, ref):
        return ref.at[pl.ds(pl.multiple_of(start, 8), size)]

    def read_at(start, size, ref):
        return ref[pl.ds(pl.multiple_of(start, 8), size), :]

    def sum_core():
        return remote(rows_at((1 - core) * 512, 512, ar), ar_core, ar_ss.at[0], ar_rs.at[0], core_peer)

    def sum_x(d):
        return remote(
            rows_at(x_peer(d) * 128, 128, s1), ar_x.at[d - 1], ar_ss.at[d], ar_rs.at[d],
            at(x_peer(d), y, z, core),
        )

    def sum_y():
        return remote(rows_at((1 - y) * 64, 64, s2), ar_y, ar_ss.at[4], ar_rs.at[4], y_peer)

    def sum_z(d):
        return remote(
            rows_at(z_peer(d) * 8, 8, s3), ar_z.at[d - 1], ar_ss.at[4 + d], ar_rs.at[4 + d],
            at(x, y, z_peer(d), core),
        )

    base_core = core * 512
    base_x = base_core + x * 128
    base_y = base_x + y * 64
    base_z = base_y + z * 8

    def share(base, size, n, device):
        return remote(rows_at(base, size, ag), rows_at(base, size, ag), ag_ss.at[n], ag_rs.at[n], device)

    def share_z(d):
        return share(base_z, 8, d - 1, at(x, y, z_peer(d), core))

    def share_y():
        return share(base_y, 64, 7, y_peer)

    def share_x(d):
        return share(base_x, 128, 7 + d, at(x_peer(d), y, z, core))

    def share_core():
        return share(base_core, 512, 11, core_peer)

    def landed_z(d):
        peer = lax.rem(z + Z - d, Z)
        return share(base_y + peer * 8, 8, d - 1, mate)

    def landed_y():
        return share(base_x + (1 - y) * 64, 64, 7, mate)

    def landed_x(d):
        peer = lax.rem(x + X - d, X)
        return share(base_core + peer * 128, 128, 7 + d, mate)

    def landed_core():
        return share((1 - core) * 512, 512, 11, mate)

    def point0():
        sum_core().start()

    def point1():
        sum_core().wait_recv()
        s1[...] = read_at(base_core, 512, ar) + ar_core[...]
        for d in range(1, X):
            sum_x(d).start()

    def point2():
        total = read_at(x * 128, 128, s1)
        for d in range(1, X):
            sum_x(d).wait_recv()
            total = total + ar_x[d - 1]
        s2[...] = total
        sum_y().start()

    def point3():
        sum_y().wait_recv()
        s3[...] = read_at(y * 64, 64, s2) + ar_y[...]
        for d in range(1, Z):
            sum_z(d).start()

    def point4():
        total = read_at(z * 8, 8, s3)
        for d in range(1, Z):
            sum_z(d).wait_recv()
            total = total + ar_z[d - 1]
        ag[pl.ds(pl.multiple_of(base_z, 8), 8), :] = total
        for d in range(1, Z):
            share_z(d).start()

    def point5():
        for d in range(1, Z):
            landed_z(d).wait_recv()
        share_y().start()

    def point6():
        landed_y().wait_recv()
        for d in range(1, X):
            share_x(d).start()

    def point7():
        for d in range(1, X):
            landed_x(d).wait_recv()
        share_core().start()

    wgrad_copy = pltpu.make_async_copy(wg, wgrad_out, local_sem.at[5])

    def point8():
        landed_core().wait_recv()
        for h in range(2):
            wg[:, h * LANES:(h + 1) * LANES] = ag[pl.ds(h * 512, 512), :]
        wgrad_copy.start()

    each(GRID, lambda j: z_step(0, j))
    for c in range(2):
        weight_part(agg, feat, c)
        weight_part(agg_far, other, c)
    point0()
    each(4, lambda j: z_step(1, j))
    point1()
    each(4, lambda j: z_step(1, j), 4)
    point2()
    each(4, lambda j: z_step(2, j))
    point3()
    each(4, lambda j: z_step(2, j), 4)
    point4()
    each(2, last_step)
    point5()
    each(2, last_step, 2)
    point6()
    each(2, last_step, 4)
    point7()
    each(2, last_step, 6)
    point8()

    def finish(j):
        f_copy(j).wait_recv()
        f_own[j] += f_recv[j]
        rows = pl.ds(pl.multiple_of(j * LANES, LANES), LANES)
        pltpu.make_async_copy(f_own.at[j], grad_out.at[rows], local_sem.at[6 + j]).start()

    each(GRID, finish)

    for c in range(2):
        for w in range(1, SLOTS):
            for j in range(4):
                fwd_copy(w, c, j).wait_send()
        for i in range(2):
            y_copy(c, i).wait_send()

    def sent(j):
        for s in range(3):
            z_copy(s, j).wait_send()
        f_copy(j).wait_send()

    each(GRID, sent)
    sum_core().wait_send()
    sum_y().wait_send()
    share_core().wait_send()
    share_y().wait_send()
    for d in range(1, X):
        sum_x(d).wait_send()
        share_x(d).wait_send()
    for d in range(1, Z):
        sum_z(d).wait_send()
        share_z(d).wait_send()
    act_copy.wait()
    wgrad_copy.wait()

    def written(j):
        rows = pl.ds(pl.multiple_of(j * LANES, LANES), LANES)
        pltpu.make_async_copy(f_own.at[j], grad_out.at[rows], local_sem.at[6 + j]).wait()

    each(GRID, written)


def body(features, weight, cotangent, block_rows, block_cols, block_counts, block_values):
    order = jnp.arange(CAP, dtype=jnp.int32)
    live = order[None, :] < block_counts[0][:, None]
    place = jnp.where(live, block_rows[0] * GRID + block_cols[0], -1)
    hit = place[:, None, :] == jnp.arange(GRID * GRID, dtype=jnp.int32)[None, :, None]
    table = jnp.max(jnp.where(hit, order[None, None, :], -1), axis=2).reshape(-1)
    vmem = pltpu.VMEM
    dma = pltpu.SemaphoreType.DMA
    anywhere = pl.BlockSpec(memory_space=pl.ANY)
    return pl.pallas_call(
        kernel,
        out_shape=(
            jax.ShapeDtypeStruct((ROWS, HALF), F32),
            jax.ShapeDtypeStruct((ROWS, HALF), F32),
            jax.ShapeDtypeStruct((2 * HALF, HALF), F32),
        ),
        in_specs=[pl.BlockSpec(memory_space=pltpu.SMEM)] + [anywhere] * 4,
        out_specs=(anywhere,) * 3,
        scratch_shapes=[
            vmem((SLOTS * CAP, LANES, LANES), F32),
            vmem((SLOTS * GRID, ROWS, LANES), BF16),
            vmem((SLOTS * GRID, ROWS, LANES), BF16),
            vmem((ROWS, HALF), F32),
            vmem((2 * HALF, HALF), F32),
            vmem((2, HALF, HALF), BF16),
            vmem((2, HALF, HALF), BF16),
            vmem((2, HALF, HALF), BF16),
            vmem((2, HALF, HALF), BF16),
            vmem((ROWS, HALF), F32),
            vmem((24, 256, LANES), F32),
            vmem((2, ROWS, LANES), F32),
            vmem((2, ROWS, LANES), F32),
            vmem((ROWS, HALF), F32),
            vmem((ROWS, HALF), F32),
            vmem((HALF, ROWS), BF16),
            vmem((HALF, ROWS), BF16),
            vmem((3 * GRID, HALF, LANES), F32),
            vmem((3 * GRID, HALF, LANES), F32),
            vmem((GRID, LANES, HALF), F32),
            vmem((GRID, LANES, HALF), F32),
            vmem((GRID, LANES, HALF), F32),
            vmem((1024, LANES), F32),
            vmem((512, LANES), F32),
            vmem((512, LANES), F32),
            vmem((3, 128, LANES), F32),
            vmem((128, LANES), F32),
            vmem((64, LANES), F32),
            vmem((64, LANES), F32),
            vmem((7, 8, LANES), F32),
            vmem((1024, LANES), F32),
            vmem((2 * HALF, HALF), F32),
            dma((14,)),
            dma((24,)), dma((24,)),
            dma((4,)), dma((4,)),
            dma((24,)), dma((24,)),
            dma((8,)), dma((8,)),
            dma((12,)), dma((12,)),
            dma((12,)), dma((12,)),
        ],
        compiler_params=pltpu.CompilerParams(
            collective_id=0, has_side_effects=True, vmem_limit_bytes=56 * 2**20
        ),
        cost_estimate=pl.CostEstimate(flops=16 * 10**9, bytes_accessed=12 * 2**20, transcendentals=ROWS * HALF),
        name="layer",
    )(table, features, weight, cotangent, block_values.reshape(SLOTS * CAP, LANES, LANES))


def solution(mesh):
    in_specs = (
        P("dom", "feat"),
        P(None, "feat"),
        P("dom", "feat"),
        P("dom", None, None),
        P("dom", None, None),
        P("dom", None),
        P("dom", None, None, None, None),
    )
    out_specs = (P("dom", "feat"), P("dom", "feat"), P(None, "feat"))
    return jax.shard_map(body, mesh=mesh, in_specs=in_specs, out_specs=out_specs, check_vma=False)
```

time: 1420 us -> 144 us (0.10)
  the two profiles are of different devices: /device:TPU:22 before, /device:TPU:1 now
where the time goes in v1:
time: 144 us
  Pallas kernels  135 us (94%)
  local copies, waits for them, and re-layouts  7.04 us (5%)
    pallas_call x1, Pallas kernels, body(): pl.pallas_call(kernel, out_shape=(jax.ShapeDtypeStruct((ROWS, HALF), F32)...  135 us
    unnamed x3, local copies, waits for them, and re-layouts  6.39 us

profile of v1, /device:TPU:1, one launch (start us, length us, event | category | flops | bytes accessed | tf_op | source)
XLA Modules:
  0.0 143.5 jit_solution(709978264721626837)
XLA Ops:
  0.6 0.8 bitcast_select_fusion
  1.4 0.1 select_reduce_fusion
  1.5 0.6 reshape.46.table
  2.1 135.0 %layer.1 = (f32[1024,256]{1,0:T(8,128)}, f32[1024,256]{1,0:T(8,128)}, f32[512,256]{1,0:T(8,128)}) custom-call(s32[256]{0:T(256)} %reshape.46.table, f32[1024,256]{1,0:T(8,128)} %features.1, f32[512,256]{1,0:T(8,128)} %weight.1, f32[1024,256]{1,0:T(8,128)} %cotangent.1, f32[96,128,128]{2,1,0:T(8,128)} %bitcast.5), custom_call_target="tpu_custom_call" | custom-call | flops 16000000000 | bytes 12582912 | tf_op jit(solution)/shard_map/layer/pallas_call | solution.py:463
  137.2 2.3 %copy.13 = f32[1024,256]{1,0:T(8,128)} copy(f32[1024,256]{1,0:T(8,128)} %get-tuple-element.6) | data formatting | bytes 2097152
  139.4 2.3 %copy.14 = f32[1024,256]{1,0:T(8,128)} copy(f32[1024,256]{1,0:T(8,128)} %get-tuple-element.7) | data formatting | bytes 2097152
  141.7 1.9 %copy.15 = f32[512,256]{1,0:T(8,128)} copy(f32[512,256]{1,0:T(8,128)} %get-tuple-element.8) | data formatting | bytes 1048576

commit v2 on v1

--- a/solution.py
+++ b/solution.py
@@ -43,7 +43,9 @@
     fwd, agg, agg_far, pre, act, pgt_hi, pgt_lo,
     z_send, z_recv, f_send, f_recv, f_own,
     ar, ar_core, s1, ar_x, s2, ar_y, s3, ar_z, ag, wg,
+    fwd_relay, z_relay,
     local_sem, fwd_ss, fwd_rs, y_ss, y_rs, z_ss, z_rs, f_ss, f_rs,
+    fwd_in, fwd_on, z_in, z_on,
     ar_ss, ar_rs, ag_ss, ag_rs,
 ):
     me = lax.axis_index("dom")
@@ -61,6 +63,15 @@
         return (((x_ * Y + y_) * Z + z_) * 2 + core_, feat)
 
     core_peer = at(x, y, z, 1 - core)
+    x_next, x_before = lax.rem(x + y, X), lax.rem(x + y + X - 1, X)
+    first_z, last_z = z == 0, z == Z - 1
+    is_odd, is_even = core == 1, core == 0
+    wraps_up, wraps_down = is_odd & last_z, is_even & first_z
+    relays_up, relays_down = is_even & last_z, is_odd & first_z
+    up_relay = at(x_next, 1 - y, Z - 1, 0)
+    up_relay_on = at(x, y, 0, 0)
+    down_relay = at(x_before, 1 - y, 0, 1)
+    down_relay_on = at(x, y, Z - 1, 1)
     y_peer = at(x, 1 - y, z, core)
 
     def x_peer(d):
@@ -82,6 +93,7 @@
     partners = [up, down, mate, y_peer]
     partners += [at(x_peer(d), y, z, core) for d in range(1, X)]
     partners += [at(x, y, z_peer(d), core) for d in range(1, Z)]
+    partners += [at(x_next, 1 - y, z, 1 - core), at(x_before, 1 - y, z, 1 - core)]
     for partner in partners:
         pl.semaphore_signal(barrier, inc=1, device_id=partner, device_id_type=MESH)
     pl.semaphore_wait(barrier, len(partners))
@@ -97,6 +109,35 @@
             src = fwd.at[fwd_at(w - 1, c, j)]
         return remote(src, fwd.at[i], fwd_ss.at[i], fwd_rs.at[i], up)
 
+    def fwd_detour(w, c, j):
+        i = fwd_at(w, c, j)
+        if w == 1:
+            src = features.at[pl.ds(j * 256, 256), pl.ds(c * LANES, LANES)]
+        else:
+            src = fwd.at[fwd_at(w - 1, c, j)]
+        n = fwd_at(w, c, 0) // 2 + j // 2
+        return remote(src, fwd_relay.at[n], fwd_ss.at[i], fwd_in.at[n], up_relay)
+
+    def fwd_resend(w, c, j):
+        i = fwd_at(w, c, j)
+        n = fwd_at(w, c, 0) // 2 + j // 2
+        return remote(fwd_relay.at[n], fwd.at[i], fwd_on.at[n], fwd_rs.at[i], up_relay_on)
+
+    def fwd_start(w, c, j):
+        if j % 2 == 0:
+            fwd_copy(w, c, j).start()
+        else:
+            pl.when(wraps_up)(lambda: fwd_detour(w, c, j).start())
+            pl.when(jnp.logical_not(wraps_up))(lambda: fwd_copy(w, c, j).start())
+
+    def relay_up(w, c):
+        def run():
+            for j in (1, 3):
+                fwd_detour(w, c, j).wait_recv()
+                fwd_resend(w, c, j).start()
+
+        pl.when(relays_up)(run)
+
     def each(n, body, start=0):
         def step(j, carry):
             body(j)
@@ -106,14 +147,12 @@
 
     def send_own(c):
         for j in range(4):
-            fwd_copy(1, c, j).start()
+            fwd_start(1, c, j)
 
     def pass_on(w, c):
-        def body(j):
+        for j in range(4):
             fwd_copy(w, c, j).wait_recv()
-            fwd_copy(w + 1, c, j).start()
-
-        each(4, body)
+            fwd_start(w + 1, c, j)
 
     def densify(w):
         def body(r):
@@ -180,19 +219,25 @@
     loads[0].wait()
     densify(0)
     densify(1)
+    relay_up(1, 0)
     pass_on(1, 0)
     densify(2)
+    densify(3)
+    relay_up(2, 0)
     pass_on(2, 0)
     send_own(1)
-    densify(3)
+    relay_up(3, 0)
     loads[1].wait()
     gather_own(0)
     gather_slot(1, 0, False)
+    relay_up(1, 1)
     gather_slot(2, 0, False)
+    gather_last(0)
+    relay_up(2, 1)
     pass_on(1, 1)
-    gather_last(0)
+    gather_own(1)
+    relay_up(3, 1)
     pass_on(2, 1)
-    gather_own(1)
     gather_slot(1, 1, False)
     gather_slot(2, 1, False)
 
@@ -247,19 +292,43 @@
         n = s * GRID + j
         return remote(z_send.at[n], z_recv.at[n], z_ss.at[n], z_rs.at[n], down)
 
+    def z_detour(s, j):
+        n = s * GRID + j
+        k = s * (GRID // 2) + j // 2
+        return remote(z_send.at[n], z_relay.at[k], z_ss.at[n], z_in.at[k], down_relay)
+
+    def z_resend(s, j):
+        n = s * GRID + j
+        k = s * (GRID // 2) + j // 2
+        return remote(z_relay.at[k], z_recv.at[n], z_on.at[k], z_rs.at[n], down_relay_on)
+
+    def z_start(s, j):
+        detour = wraps_down & (lax.rem(j, 2) == 1)
+        pl.when(detour)(lambda: z_detour(s, j).start())
+        pl.when(jnp.logical_not(detour))(lambda: z_copy(s, j).start())
+
+    def relay_down(s, j):
+        def run():
+            z_detour(s, j).wait_recv()
+            z_resend(s, j).start()
+
+        pl.when(relays_down & (lax.rem(j, 2) == 1))(run)
+
     def z_step(s, j):
         value = term(3 - s, j)
         if s > 0:
+            relay_down(s - 1, j)
             z_copy(s - 1, j).wait_recv()
             value = value + z_recv[(s - 1) * GRID + j]
         z_send[s * GRID + j] = value
-        z_copy(s, j).start()
+        z_start(s, j)
 
     def f_copy(j):
         return remote(f_send.at[j], f_recv.at[j], f_ss.at[j], f_rs.at[j], mate)
 
     def last_step(j):
         value = term(0, j)
+        relay_down(2, j)
         z_copy(2, j).wait_recv()
         value = value + z_recv[2 * GRID + j]
         parts = split(value.T)
@@ -422,12 +491,14 @@
         for w in range(1, SLOTS):
             for j in range(4):
                 fwd_copy(w, c, j).wait_send()
+            pl.when(relays_up)(lambda w=w, c=c: [fwd_resend(w, c, j).wait_send() for j in (1, 3)] and None)
         for i in range(2):
             y_copy(c, i).wait_send()
 
     def sent(j):
         for s in range(3):
             z_copy(s, j).wait_send()
+            pl.when(relays_down & (lax.rem(j, 2) == 1))(lambda s=s: z_resend(s, j).wait_send())
         f_copy(j).wait_send()
 
     each(GRID, sent)
@@ -451,6 +522,24 @@
     each(GRID, written)
 
 
+def copy_kernel(a_in, b_in, c_in, a_out, b_out, c_out, a, b, c, sems):
+    groups = ((a_in, a, a_out), (b_in, b, b_out), (c_in, c, c_out))
+    reads, writes = [], []
+    for i, (src, mid, dst) in enumerate(groups):
+        size = src.shape[0] // 4
+        for k in range(4):
+            rows = pl.ds(k * size, size)
+            reads.append(pltpu.make_async_copy(src.at[rows], mid.at[rows], sems.at[i * 4 + k]))
+            writes.append(pltpu.make_async_copy(mid.at[rows], dst.at[rows], sems.at[12 + i * 4 + k]))
+    for read in reads:
+        read.start()
+    for read, write in zip(reads, writes):
+        read.wait()
+        write.start()
+    for write in writes:
+        write.wait()
+
+
 def body(features, weight, cotangent, block_rows, block_cols, block_counts, block_values):
     order = jnp.arange(CAP, dtype=jnp.int32)
     live = order[None, :] < block_counts[0][:, None]
@@ -460,7 +549,7 @@
     vmem = pltpu.VMEM
     dma = pltpu.SemaphoreType.DMA
     anywhere = pl.BlockSpec(memory_space=pl.ANY)
-    return pl.pallas_call(
+    results = pl.pallas_call(
         kernel,
         out_shape=(
             jax.ShapeDtypeStruct((ROWS, HALF), F32),
@@ -502,11 +591,14 @@
             vmem((7, 8, LANES), F32),
             vmem((1024, LANES), F32),
             vmem((2 * HALF, HALF), F32),
+            vmem((12, 256, LANES), F32),
+            vmem((12, HALF, LANES), F32),
             dma((14,)),
             dma((24,)), dma((24,)),
             dma((4,)), dma((4,)),
             dma((24,)), dma((24,)),
             dma((8,)), dma((8,)),
+            dma((12,)), dma((12,)), dma((12,)), dma((12,)),
             dma((12,)), dma((12,)),
             dma((12,)), dma((12,)),
         ],
@@ -516,6 +608,14 @@
         cost_estimate=pl.CostEstimate(flops=16 * 10**9, bytes_accessed=12 * 2**20, transcendentals=ROWS * HALF),
         name="layer",
     )(table, features, weight, cotangent, block_values.reshape(SLOTS * CAP, LANES, LANES))
+    return pl.pallas_call(
+        copy_kernel,
+        out_shape=tuple(jax.ShapeDtypeStruct(r.shape, F32) for r in results),
+        in_specs=[anywhere] * 3,
+        out_specs=(anywhere,) * 3,
+        scratch_shapes=[vmem(r.shape, F32) for r in results] + [dma((24,))],
+        name="results",
+    )(*results)
 
 
 def solution(mesh):

time: 144 us -> 134 us (0.931)
  the two profiles are of different devices: /device:TPU:1 before, /device:TPU:22 now
where the time goes in v2:
time: 134 us; the launch traced here: 133 us
  Pallas kernels  131 us (98%)
    pallas_call x1, Pallas kernels, body(): pl.pallas_call(kernel, out_shape=(jax.ShapeDtypeStruct((ROWS, HALF), F32)...  128 us

profile of v2, /device:TPU:22, one launch (start us, length us, event | category | flops | bytes accessed | tf_op | source)
XLA Modules:
  0.0 133.2 jit_solution(10614839444086598230)
XLA Ops:
  0.6 0.8 bitcast_select_fusion
  1.4 0.1 select_reduce_fusion
  1.5 0.6 reshape.46.table
  2.1 128.4 %layer.1 = (f32[1024,256]{1,0:T(8,128)}, f32[1024,256]{1,0:T(8,128)}, f32[512,256]{1,0:T(8,128)}) custom-call(s32[256]{0:T(256)} %reshape.46.table, f32[1024,256]{1,0:T(8,128)} %features.1, f32[512,256]{1,0:T(8,128)} %weight.1, f32[1024,256]{1,0:T(8,128)} %cotangent.1, f32[96,128,128]{2,1,0:T(8,128)} %bitcast.5), custom_call_target="tpu_custom_call" | custom-call | flops 16000000000 | bytes 12582912 | tf_op jit(solution)/shard_map/layer/pallas_call | solution.py:552
  130.5 2.6 %results.1 = (f32[1024,256]{1,0:T(8,128)}, f32[1024,256]{1,0:T(8,128)}, f32[512,256]{1,0:T(8,128)}) custom-call(f32[1024,256]{1,0:T(8,128)} %get-tuple-element.6.a_in, f32[1024,256]{1,0:T(8,128)} %get-tuple-element.7.b_in, f32[512,256]{1,0:T(8,128)} %get-tuple-element.8.c_in), custom_call_target="tpu_custom_call" | custom-call | tf_op jit(solution)/shard_map/results/pallas_call | solution.py:611

commit v3 on v2

--- a/solution.py
+++ b/solution.py
@@ -40,9 +40,9 @@
     table, features, weight, cotangent, blocks_in,
     act_out, grad_out, wgrad_out,
     blocks, adj_hi, adj_lo, own, w_raw, w_hi, w_lo, wt_hi, wt_lo, cot,
-    fwd, agg, agg_far, pre, act, pgt_hi, pgt_lo,
+    fwd, side_hi, side_lo, agg, agg_far, pre, act, pgt,
     z_send, z_recv, f_send, f_recv, f_own,
-    ar, ar_core, s1, ar_x, s2, ar_y, s3, ar_z, ag, wg,
+    ar, ar_core, s1, ar_x, s2, ar_y, s3, ar_z, ag,
     fwd_relay, z_relay,
     local_sem, fwd_ss, fwd_rs, y_ss, y_rs, z_ss, z_rs, f_ss, f_rs,
     fwd_in, fwd_on, z_in, z_on,
@@ -166,7 +166,7 @@
 
         each(GRID, body)
 
-    def gather_in(w, c, j, piece, first=False, last=None):
+    def gather_in(w, c, j, piece, last=None):
         high, low = split(piece)
         both = jnp.concatenate([high, low], axis=1)
 
@@ -180,40 +180,62 @@
             )
             wide = dot(a_hi, both)
             total = wide[:, :LANES] + wide[:, LANES:] + dot(a_lo, high)
-            if first:
-                agg[c, rows, :] = total
-            else:
-                agg[c, rows, :] += total
+            agg[c, rows, :] += total
             if last is not None:
                 last(i)
 
         each(2, body)
 
-    def gather_own(c):
-        def piece(j):
-            rows = pl.ds(pl.multiple_of(j * 256, 256), 256)
-            return own[rows, pl.ds(c * LANES, LANES)]
-
-        gather_in(0, c, 0, piece(0), first=True)
-        each(3, lambda j: gather_in(0, c, j, piece(j)), 1)
-
-    def gather_slot(w, c, wait, n=4):
+    def tile(adj, w, i):
+        rows = pl.ds(pl.multiple_of(i * 256, 256), 256)
+        return jnp.concatenate([adj[w * GRID + k, rows, :] for k in range(GRID)], axis=1)
+
+    def gather_own():
+        for c in range(2):
+            high, low = split(own[:, c * LANES:(c + 1) * LANES])
+            side_hi[:, c * LANES:(c + 1) * LANES] = high
+            side_lo[:, c * LANES:(c + 1) * LANES] = low
+
+        def body(i):
+            a_hi, a_lo = tile(adj_hi, 0, i), tile(adj_lo, 0, i)
+            total = dot(a_hi, side_hi[...]) + dot(a_hi, side_lo[...]) + dot(a_lo, side_hi[...])
+            rows = pl.ds(pl.multiple_of(i * 256, 256), 256)
+            for c in range(2):
+                agg[c, rows, :] = total[:, c * LANES:(c + 1) * LANES]
+
+        each(4, body)
+
+    def gather_slot(w, c):
+        for j in range(4):
+            high, low = split(fwd[fwd_at(w, c, j)])
+            side_hi[j * 256:(j + 1) * 256, :LANES] = high
+            side_hi[j * 256:(j + 1) * 256, LANES:] = low
+
+        def body(i):
+            wide = dot(tile(adj_hi, w, i), side_hi[...])
+            rest = dot(tile(adj_lo, w, i), side_hi[:, :LANES])
+            rows = pl.ds(pl.multiple_of(i * 256, 256), 256)
+            agg[c, rows, :] += wide[:, :LANES] + wide[:, LANES:] + rest
+
+        each(4, body)
+
+    def y_copy(c, i):
+        rows = pl.ds(pl.multiple_of(i * 256, 256), 256)
+        n = c * 4 + i
+        return remote(agg.at[c, rows], agg_far.at[c, rows], y_ss.at[n], y_rs.at[n], mate)
+
+    def y_start(c, i):
+        y_copy(c, 2 * i).start()
+        y_copy(c, 2 * i + 1).start()
+
+    def gather_last(c):
         def body(j):
-            if wait:
-                fwd_copy(w, c, j).wait_recv()
-            gather_in(w, c, j, fwd[fwd_at(w, c, j)])
-
-        each(n, body)
-
-    def y_copy(c, i):
-        rows = pl.ds(pl.multiple_of(i * 512, 512), 512)
-        n = c * 2 + i
-        return remote(agg.at[c, rows], agg_far.at[c, rows], y_ss.at[n], y_rs.at[n], mate)
-
-    def gather_last(c):
-        gather_slot(3, c, True, 3)
+            fwd_copy(3, c, j).wait_recv()
+            gather_in(3, c, j, fwd[fwd_at(3, c, j)])
+
+        each(3, body)
         fwd_copy(3, c, 3).wait_recv()
-        gather_in(3, c, 3, fwd[fwd_at(3, c, 3)], last=lambda i: y_copy(c, i).start())
+        gather_in(3, c, 3, fwd[fwd_at(3, c, 3)], last=lambda i: y_start(c, i))
 
     send_own(0)
     loads[0].wait()
@@ -221,25 +243,24 @@
     densify(1)
     relay_up(1, 0)
     pass_on(1, 0)
+    send_own(1)
     densify(2)
     densify(3)
     relay_up(2, 0)
     pass_on(2, 0)
-    send_own(1)
     relay_up(3, 0)
     loads[1].wait()
-    gather_own(0)
-    gather_slot(1, 0, False)
+    gather_own()
+    gather_slot(1, 0)
     relay_up(1, 1)
-    gather_slot(2, 0, False)
+    gather_slot(2, 0)
     gather_last(0)
     relay_up(2, 1)
     pass_on(1, 1)
-    gather_own(1)
+    gather_slot(1, 1)
     relay_up(3, 1)
     pass_on(2, 1)
-    gather_slot(1, 1, False)
-    gather_slot(2, 1, False)
+    gather_slot(2, 1)
 
     loads[2].wait()
     for k in range(2):
@@ -255,7 +276,7 @@
         pre[rows, :] = dot3(split(value), (w_hi[feat], w_lo[feat]))
 
     each(4, near_part)
-    for i in range(2):
+    for i in range(4):
         y_copy(0, i).wait_recv()
 
     def far_part(c, i):
@@ -271,22 +292,29 @@
 
     def activate(i):
         rows = pl.ds(pl.multiple_of(i * 256, 256), 256)
+        y_copy(1, i).wait_recv()
         value = pre[rows, :] + far_part(1, i)
         s = jax.nn.sigmoid(value)
         act[rows, :] = value * s
         grad = cot[rows, :] * (s + value * s * (1.0 - s))
-        pgt_hi[:, rows], pgt_lo[:, rows] = split(grad.T)
-
-    for i in range(2):
-        y_copy(1, i).wait_recv()
-        each(2, activate, 2 * i)
+        pgt[:HALF, rows], pgt[HALF:, rows] = split(grad.T)
+
+    each(4, activate)
     act_copy = pltpu.make_async_copy(act, act_out, local_sem.at[4])
     act_copy.start()
 
-    def term(w, j):
+    def times_pgt(high, low):
+        both = dot(pgt[...], high)
+        return both[:HALF] + both[HALF:] + dot(pgt[:HALF, :], low)
+
+    def term(w, j, count):
         n = w * GRID + j
-        high, low = pgt_hi[...], pgt_lo[...]
-        return dot(high, adj_hi[n]) + dot(low, adj_hi[n]) + dot(high, adj_lo[n])
+        if count == 1:
+            return times_pgt(adj_hi[n], adj_lo[n])
+        return times_pgt(
+            jnp.concatenate([adj_hi[n], adj_hi[n + 1]], axis=1),
+            jnp.concatenate([adj_lo[n], adj_lo[n + 1]], axis=1),
+        )
 
     def z_copy(s, j):
         n = s * GRID + j
@@ -302,47 +330,60 @@
         k = s * (GRID // 2) + j // 2
         return remote(z_relay.at[k], z_recv.at[n], z_on.at[k], z_rs.at[n], down_relay_on)
 
-    def z_start(s, j):
-        detour = wraps_down & (lax.rem(j, 2) == 1)
-        pl.when(detour)(lambda: z_detour(s, j).start())
-        pl.when(jnp.logical_not(detour))(lambda: z_copy(s, j).start())
-
-    def relay_down(s, j):
-        def run():
-            z_detour(s, j).wait_recv()
-            z_resend(s, j).start()
-
-        pl.when(relays_down & (lax.rem(j, 2) == 1))(run)
-
-    def z_step(s, j):
-        value = term(3 - s, j)
-        if s > 0:
-            relay_down(s - 1, j)
-            z_copy(s - 1, j).wait_recv()
-            value = value + z_recv[(s - 1) * GRID + j]
-        z_send[s * GRID + j] = value
-        z_start(s, j)
+    def z_start(s, j, odd):
+        if odd:
+            pl.when(wraps_down)(lambda: z_detour(s, j).start())
+            pl.when(jnp.logical_not(wraps_down))(lambda: z_copy(s, j).start())
+        else:
+            z_copy(s, j).start()
+
+    def carried(s, j, odd):
+        if odd:
+            def run():
+                z_detour(s, j).wait_recv()
+                z_resend(s, j).start()
+
+            pl.when(relays_down)(run)
+        z_copy(s, j).wait_recv()
+        return z_recv[s * GRID + j]
+
+    def z_step(s, pair):
+        value = term(3 - s, 2 * pair, 2)
+        for h in range(2):
+            j = 2 * pair + h
+            part = value[:, h * LANES:(h + 1) * LANES]
+            if s > 0:
+                part = part + carried(s - 1, j, h == 1)
+            z_send[s * GRID + j] = part
+            z_start(s, j, h == 1)
 
     def f_copy(j):
         return remote(f_send.at[j], f_recv.at[j], f_ss.at[j], f_rs.at[j], mate)
 
-    def last_step(j):
-        value = term(0, j)
-        relay_down(2, j)
-        z_copy(2, j).wait_recv()
-        value = value + z_recv[2 * GRID + j]
-        parts = split(value.T)
-        f_send[j] = dot3(parts, (wt_hi[other], wt_lo[other]))
-        f_copy(j).start()
-        f_own[j] = dot3(parts, (wt_hi[feat], wt_lo[feat]))
+    def last_step(start, odds):
+        count = len(odds)
+        value = term(0, start, count)
+        sums = [
+            value[:, h * LANES:(h + 1) * LANES] + carried(2, start + h, odd)
+            for h, odd in enumerate(odds)
+        ]
+        parts = split(jnp.concatenate(sums, axis=1).T)
+        far = dot3(parts, (wt_hi[other], wt_lo[other]))
+        for h in range(count):
+            f_send[start + h] = far[h * LANES:(h + 1) * LANES]
+            f_copy(start + h).start()
+        near = dot3(parts, (wt_hi[feat], wt_lo[feat]))
+        for h in range(count):
+            f_own[start + h] = near[h * LANES:(h + 1) * LANES]
 
     scale = F32(1.0 / math.sqrt(ROWS * PARTS))
 
-    def weight_part(source, half, c):
-        grad = dot3((pgt_hi[...], pgt_lo[...]), split(source[c])).T * scale
+    def weight_part(source, half):
+        high, low = split(jnp.concatenate([source[0], source[1]], axis=1))
+        grad = times_pgt(high, low).T * scale
         for h in range(2):
-            start = pl.multiple_of(h * 512 + half * HALF + c * LANES, LANES)
-            ar[pl.ds(start, LANES), :] = grad[:, h * LANES:(h + 1) * LANES]
+            start = pl.multiple_of(h * 512 + half * HALF, HALF)
+            ar[pl.ds(start, HALF), :] = grad[:, h * LANES:(h + 1) * LANES]
 
     def rows_at(start, size, ref):
         return ref.at[pl.ds(pl.multiple_of(start, 8), size)]
@@ -449,35 +490,55 @@
             landed_x(d).wait_recv()
         share_core().start()
 
-    wgrad_copy = pltpu.make_async_copy(wg, wgrad_out, local_sem.at[5])
+    wgrad_copies = [
+        pltpu.make_async_copy(
+            ag.at[pl.ds(h * 512, 512)], wgrad_out.at[:, pl.ds(h * LANES, LANES)], local_sem.at[(5, 14)[h]]
+        )
+        for h in range(2)
+    ]
 
     def point8():
         landed_core().wait_recv()
-        for h in range(2):
-            wg[:, h * LANES:(h + 1) * LANES] = ag[pl.ds(h * 512, 512), :]
-        wgrad_copy.start()
-
-    each(GRID, lambda j: z_step(0, j))
-    for c in range(2):
-        weight_part(agg, feat, c)
-        weight_part(agg_far, other, c)
+        for copy in wgrad_copies:
+            copy.start()
+
+    late = first_z | (z >= Z - 2)
+    soon = jnp.logical_not(late)
+
+    def after(i, points, where):
+        for k, point in points.items():
+            pl.when((i == k) & where)(point)
+
+    def third(i):
+        z_step(2, i)
+        after(i, {2: point4, 3: point5}, is_odd & late)
+        after(i, {3: point4}, is_even & late)
+
+    def fourth(i):
+        last_step(2 * i, (False, True))
+        after(i, {0: point6, 1: point7}, is_odd & late)
+        after(i, {0: point5, 1: point6, 2: point7}, is_even & late)
+        after(i, {0: point4, 1: point5, 2: point6}, is_odd & soon)
+
+    def even_end():
+        point4()
+        point5()
+        point6()
+
+    each(4, lambda i: z_step(0, i))
+    weight_part(agg, feat)
+    weight_part(agg_far, other)
     point0()
-    each(4, lambda j: z_step(1, j))
     point1()
-    each(4, lambda j: z_step(1, j), 4)
     point2()
-    each(4, lambda j: z_step(2, j))
+    each(4, lambda i: z_step(1, i))
     point3()
-    each(4, lambda j: z_step(2, j), 4)
-    point4()
-    each(2, last_step)
-    point5()
-    each(2, last_step, 2)
-    point6()
-    each(2, last_step, 4)
-    point7()
-    each(2, last_step, 6)
-    point8()
+    each(4, third)
+    each(3, fourth)
+    last_step(6, (False,))
+    last_step(7, (True,))
+    pl.when(is_even & soon)(even_end)
+    pl.when(soon)(point7)
 
     def finish(j):
         f_copy(j).wait_recv()
@@ -486,13 +547,14 @@
         pltpu.make_async_copy(f_own.at[j], grad_out.at[rows], local_sem.at[6 + j]).start()
 
     each(GRID, finish)
+    point8()
 
     for c in range(2):
         for w in range(1, SLOTS):
             for j in range(4):
                 fwd_copy(w, c, j).wait_send()
             pl.when(relays_up)(lambda w=w, c=c: [fwd_resend(w, c, j).wait_send() for j in (1, 3)] and None)
-        for i in range(2):
+        for i in range(4):
             y_copy(c, i).wait_send()
 
     def sent(j):
@@ -513,7 +575,8 @@
         sum_z(d).wait_send()
         share_z(d).wait_send()
     act_copy.wait()
-    wgrad_copy.wait()
+    for copy in wgrad_copies:
+        copy.wait()
 
     def written(j):
         rows = pl.ds(pl.multiple_of(j * LANES, LANES), LANES)
@@ -570,12 +633,13 @@
             vmem((2, HALF, HALF), BF16),
             vmem((ROWS, HALF), F32),
             vmem((24, 256, LANES), F32),
+            vmem((ROWS, HALF), BF16),
+            vmem((ROWS, HALF), BF16),
             vmem((2, ROWS, LANES), F32),
             vmem((2, ROWS, LANES), F32),
             vmem((ROWS, HALF), F32),
             vmem((ROWS, HALF), F32),
-            vmem((HALF, ROWS), BF16),
-            vmem((HALF, ROWS), BF16),
+            vmem((2 * HALF, ROWS), BF16),
             vmem((3 * GRID, HALF, LANES), F32),
             vmem((3 * GRID, HALF, LANES), F32),
             vmem((GRID, LANES, HALF), F32),
@@ -590,12 +654,11 @@
             vmem((64, LANES), F32),
             vmem((7, 8, LANES), F32),
             vmem((1024, LANES), F32),
-            vmem((2 * HALF, HALF), F32),
             vmem((12, 256, LANES), F32),
             vmem((12, HALF, LANES), F32),
-            dma((14,)),
+            dma((15,)),
             dma((24,)), dma((24,)),
-            dma((4,)), dma((4,)),
+            dma((8,)), dma((8,)),
             dma((24,)), dma((24,)),
             dma((8,)), dma((8,)),
             dma((12,)), dma((12,)), dma((12,)), dma((12,)),

time: 134 us -> 127 us (0.948)
  Pallas kernels: 131 us -> 124 us
    pallas_call x1, Pallas kernels: 128 us -> 122 us  [body(): pl.pallas_call(kernel, out_shape=(jax.ShapeDtypeStruct((ROWS, HALF), F32)...]
where the time goes in v3:
time: 127 us; the launch traced here: 126 us
  Pallas kernels  124 us (98%)
    pallas_call x1, Pallas kernels, body(): pl.pallas_call(kernel, out_shape=(jax.ShapeDtypeStruct((ROWS, HALF), F32)...  122 us
    pallas_call x1, Pallas kernels, body(): pl.pallas_call(copy_kernel, out_shape=tuple((jax.ShapeDtypeStruct(r.shape...  2.63 us

profile of v3, /device:TPU:22, one launch (start us, length us, event | category | flops | bytes accessed | tf_op | source)
XLA Modules:
  0.0 126.4 jit_solution(1639101207493569933)
XLA Ops:
  0.6 0.8 bitcast_select_fusion
  1.4 0.1 select_reduce_fusion
  1.5 0.6 reshape.46.table
  2.1 121.6 %layer.1 = (f32[1024,256]{1,0:T(8,128)}, f32[1024,256]{1,0:T(8,128)}, f32[512,256]{1,0:T(8,128)}) custom-call(s32[256]{0:T(256)} %reshape.46.table, f32[1024,256]{1,0:T(8,128)} %features.1, f32[512,256]{1,0:T(8,128)} %weight.1, f32[1024,256]{1,0:T(8,128)} %cotangent.1, f32[96,128,128]{2,1,0:T(8,128)} %bitcast.5), custom_call_target="tpu_custom_call" | custom-call | flops 16000000000 | bytes 12582912 | tf_op jit(solution)/shard_map/layer/pallas_call | solution.py:615
  123.7 2.6 %results.1 = (f32[1024,256]{1,0:T(8,128)}, f32[1024,256]{1,0:T(8,128)}, f32[512,256]{1,0:T(8,128)}) custom-call(f32[1024,256]{1,0:T(8,128)} %get-tuple-element.6.a_in, f32[1024,256]{1,0:T(8,128)} %get-tuple-element.7.b_in, f32[512,256]{1,0:T(8,128)} %get-tuple-element.8.c_in), custom_call_target="tpu_custom_call" | custom-call | tf_op jit(solution)/shard_map/results/pallas_call | solution.py:674

commit v4 on v3

--- a/solution.py
+++ b/solution.py
@@ -511,6 +511,8 @@
 
     def third(i):
         z_step(2, i)
+        after(i, {1: point3}, is_even)
+        after(i, {0: point3}, is_odd)
         after(i, {2: point4, 3: point5}, is_odd & late)
         after(i, {3: point4}, is_even & late)
 
@@ -525,14 +527,20 @@
         point5()
         point6()
 
+    def second(i):
+        z_step(1, i)
+        after(i, {1: point1, 3: point2}, is_odd)
+
+    def both12():
+        point1()
+        point2()
+
     each(4, lambda i: z_step(0, i))
     weight_part(agg, feat)
     weight_part(agg_far, other)
     point0()
-    point1()
-    point2()
-    each(4, lambda i: z_step(1, i))
-    point3()
+    each(4, second)
+    pl.when(is_even)(both12)
     each(4, third)
     each(3, fourth)
     last_step(6, (False,))

time: 127 us -> 124 us (0.976)
  Pallas kernels: 124 us -> 121 us
    pallas_call x1, Pallas kernels: 122 us -> 119 us  [body(): pl.pallas_call(kernel, out_shape=(jax.ShapeDtypeStruct((ROWS, HALF), F32)...]
where the time goes in v4:
time: 124 us
  Pallas kernels  121 us (98%)
    pallas_call x1, Pallas kernels, body(): pl.pallas_call(kernel, out_shape=(jax.ShapeDtypeStruct((ROWS, HALF), F32)...  119 us
    pallas_call x1, Pallas kernels, body(): pl.pallas_call(copy_kernel, out_shape=tuple((jax.ShapeDtypeStruct(r.shape...  2.63 us

profile of v4, /device:TPU:22, one launch (start us, length us, event | category | flops | bytes accessed | tf_op | source)
XLA Modules:
  0.0 123.6 jit_solution(1717567057077477940)
XLA Ops:
  0.6 0.8 bitcast_select_fusion
  1.4 0.1 select_reduce_fusion
  1.5 0.6 reshape.46.table
  2.1 118.8 %layer.1 = (f32[1024,256]{1,0:T(8,128)}, f32[1024,256]{1,0:T(8,128)}, f32[512,256]{1,0:T(8,128)}) custom-call(s32[256]{0:T(256)} %reshape.46.table, f32[1024,256]{1,0:T(8,128)} %features.1, f32[512,256]{1,0:T(8,128)} %weight.1, f32[1024,256]{1,0:T(8,128)} %cotangent.1, f32[96,128,128]{2,1,0:T(8,128)} %bitcast.5), custom_call_target="tpu_custom_call" | custom-call | flops 16000000000 | bytes 12582912 | tf_op jit(solution)/shard_map/layer/pallas_call | solution.py:623
  120.9 2.6 %results.1 = (f32[1024,256]{1,0:T(8,128)}, f32[1024,256]{1,0:T(8,128)}, f32[512,256]{1,0:T(8,128)}) custom-call(f32[1024,256]{1,0:T(8,128)} %get-tuple-element.6.a_in, f32[1024,256]{1,0:T(8,128)} %get-tuple-element.7.b_in, f32[512,256]{1,0:T(8,128)} %get-tuple-element.8.c_in), custom_call_target="tpu_custom_call" | custom-call | tf_op jit(solution)/shard_map/results/pallas_call | solution.py:682

commit v5 on v4

--- a/solution.py
+++ b/solution.py
@@ -37,13 +37,13 @@
 
 
 def kernel(
-    table, features, weight, cotangent, blocks_in,
+    block_rows, block_cols, block_counts, features, weight, cotangent, blocks_in,
     act_out, grad_out, wgrad_out,
     blocks, adj_hi, adj_lo, own, w_raw, w_hi, w_lo, wt_hi, wt_lo, cot,
     fwd, side_hi, side_lo, agg, agg_far, pre, act, pgt,
     z_send, z_recv, f_send, f_recv, f_own,
     ar, ar_core, s1, ar_x, s2, ar_y, s3, ar_z, ag,
-    fwd_relay, z_relay,
+    fwd_relay, z_relay, place,
     local_sem, fwd_ss, fwd_rs, y_ss, y_rs, z_ss, z_rs, f_ss, f_rs,
     fwd_in, fwd_on, z_in, z_on,
     ar_ss, ar_rs, ag_ss, ag_rs,
@@ -155,10 +155,16 @@
             fwd_start(w + 1, c, j)
 
     def densify(w):
+        for k in range(CAP):
+            at_k = block_rows[0, w, k] * GRID + block_cols[0, w, k]
+            place[k] = jnp.where(k < block_counts[0, w], at_k, -1)
+
         def body(r):
             rows = pl.ds(pl.multiple_of(r * LANES, LANES), LANES)
             for c in range(GRID):
-                found = table[(w * GRID + r) * GRID + c]
+                found = jnp.int32(-1)
+                for k in range(CAP):
+                    found = jnp.where(place[k] == r * GRID + c, k, found)
                 live = jnp.where(found >= 0, 1.0, 0.0).astype(F32)
                 high, low = split(blocks[w * CAP + jnp.maximum(found, 0)] * live)
                 adj_hi[w * GRID + c, rows, :] = high
@@ -240,10 +246,10 @@
     send_own(0)
     loads[0].wait()
     densify(0)
-    densify(1)
     relay_up(1, 0)
     pass_on(1, 0)
     send_own(1)
+    densify(1)
     densify(2)
     densify(3)
     relay_up(2, 0)
@@ -612,11 +618,6 @@
 
 
 def body(features, weight, cotangent, block_rows, block_cols, block_counts, block_values):
-    order = jnp.arange(CAP, dtype=jnp.int32)
-    live = order[None, :] < block_counts[0][:, None]
-    place = jnp.where(live, block_rows[0] * GRID + block_cols[0], -1)
-    hit = place[:, None, :] == jnp.arange(GRID * GRID, dtype=jnp.int32)[None, :, None]
-    table = jnp.max(jnp.where(hit, order[None, None, :], -1), axis=2).reshape(-1)
     vmem = pltpu.VMEM
     dma = pltpu.SemaphoreType.DMA
     anywhere = pl.BlockSpec(memory_space=pl.ANY)
@@ -627,7 +628,7 @@
             jax.ShapeDtypeStruct((ROWS, HALF), F32),
             jax.ShapeDtypeStruct((2 * HALF, HALF), F32),
         ),
-        in_specs=[pl.BlockSpec(memory_space=pltpu.SMEM)] + [anywhere] * 4,
+        in_specs=[pl.BlockSpec(memory_space=pltpu.SMEM)] * 3 + [anywhere] * 4,
         out_specs=(anywhere,) * 3,
         scratch_shapes=[
             vmem((SLOTS * CAP, LANES, LANES), F32),
@@ -664,6 +665,7 @@
             vmem((1024, LANES), F32),
             vmem((12, 256, LANES), F32),
             vmem((12, HALF, LANES), F32),
+            pltpu.SMEM((CAP,), jnp.int32),
             dma((15,)),
             dma((24,)), dma((24,)),
             dma((8,)), dma((8,)),
@@ -678,7 +680,7 @@
         ),
         cost_estimate=pl.CostEstimate(flops=16 * 10**9, bytes_accessed=12 * 2**20, transcendentals=ROWS * HALF),
         name="layer",
-    )(table, features, weight, cotangent, block_values.reshape(SLOTS * CAP, LANES, LANES))
+    )(block_rows, block_cols, block_counts, features, weight, cotangent, block_values.reshape(SLOTS * CAP, LANES, LANES))
     return pl.pallas_call(
         copy_kernel,
         out_shape=tuple(jax.ShapeDtypeStruct(r.shape, F32) for r in results),

time: 124 us -> 122 us (0.984)
  no operation moved by 1% of the time
where the time goes in v5:
time: 122 us
  Pallas kernels  122 us (100%)
    pallas_call x1, Pallas kernels, body(): pl.pallas_call(kernel, out_shape=(jax.ShapeDtypeStruct((ROWS, HALF), F32)...  119 us
    pallas_call x1, Pallas kernels, body(): pl.pallas_call(copy_kernel, out_shape=tuple((jax.ShapeDtypeStruct(r.shape...  2.63 us

profile of v5, /device:TPU:22, one launch (start us, length us, event | category | flops | bytes accessed | tf_op | source)
XLA Modules:
  0.0 122.3 jit_solution(8127095763455010007)
XLA Ops:
  0.6 119.0 %layer.1 = (f32[1024,256]{1,0:T(8,128)}, f32[1024,256]{1,0:T(8,128)}, f32[512,256]{1,0:T(8,128)}) custom-call(s32[1,4,24]{2,1,0:T(4,128)} %block_rows.1, s32[1,4,24]{2,1,0:T(4,128)} %block_cols.1, s32[1,4]{1,0:T(1,128)} %block_counts.1, f32[1024,256]{1,0:T(8,128)} %features.1, f32[512,256]{1,0:T(8,128)} %weight.1, f32[1024,256]{1,0:T(8,128)} %cotangent.1, ...), custom_call_target="tpu_custom_call" | custom-call | flops 16000000000 | bytes 12582912 | tf_op jit(solution)/shard_map/layer/pallas_call | solution.py:624
  119.6 2.6 %results.1 = (f32[1024,256]{1,0:T(8,128)}, f32[1024,256]{1,0:T(8,128)}, f32[512,256]{1,0:T(8,128)}) custom-call(f32[1024,256]{1,0:T(8,128)} %get-tuple-element.6.a_in, f32[1024,256]{1,0:T(8,128)} %get-tuple-element.7.b_in, f32[512,256]{1,0:T(8,128)} %get-tuple-element.8.c_in), custom_call_target="tpu_custom_call" | custom-call | tf_op jit(solution)/shard_map/results/pallas_call | solution.py:684
